TPU v7x, 256 devices: a whole 4x4x8 slice. The times are simulated.
256 devices in a mesh: dp: 4 (over z_hi), ctx: 64 (over z_lo, y, x, core).
Axes of the slice: x: 4, y: 4, z: 8 (z_hi: 4, z_lo: 2; z = z_hi * 2 + z_lo), core: 2. Of those that a mesh axis runs over, the one named last changes fastest.
Arguments:
- queries: bfloat16 [4, 16384, 2560], P('dp', 'ctx'), may hold values from -120 to 120
- key_rows: bfloat16 [4, 16384, 512], P('dp', 'ctx'), may hold values from -6 to 6
- value_rows: bfloat16 [4, 16384, 512], P('dp', 'ctx'), may hold values from -6 to 6
- grad_out: bfloat16 [4, 16384, 2560], P('dp', 'ctx'), may hold values from -6 to 6
- doc_lengths: int32 [4, 32], P('dp'), may hold values from 1 to 1024, 16384 in all within a row
Outputs:
- attn_out: bfloat16 [4, 16384, 2560], P('dp', 'ctx')
- grad_queries: bfloat16 [4, 16384, 2560], P('dp', 'ctx')
- grad_keys: bfloat16 [4, 16384, 512], P('dp', 'ctx')
- grad_values: bfloat16 [4, 16384, 512], P('dp', 'ctx')
- bias_grad: float32 [3584], replicated
Inputs may be any that keep to these rules, and one draw needn't show every extreme that they name: `doc_lengths`: each row's 32 lengths sum to 16384, and the largest in each row is exactly 1024.
All inputs are finite; a program needn't handle non-finite values.
Results may differ from a plain program's by a relative error of at most 0.012.
The roundings to bfloat16 on the way count: a program that leaves them out, or rounds other values in their place, can miss the bound.
Values may be sent and summed in bfloat16 or wider, within the bound.
A program may use at most 128 MiB of HBM per device.

v0:
```python
import math

import jax
import jax.numpy as jnp
from jax import lax
from jax.sharding import PartitionSpec as P

KVH = 4
HD = 128
GROUP = 5
DOC_SPAN = 4


def passed_along(shard, axis, by):
    length = lax.axis_size(axis)
    pairs = [(i, i + by) for i in range(length) if 0 <= i + by < length]
    return lax.ppermute(shard, axis, pairs)


def positions_doc(positions, bounds):
    return jnp.sum((positions[:, None] >= bounds[None, :]).astype(jnp.int32), axis=1)


def window_attention(query_block, key_window, value_window, grad_block, query_pos, key_pos, bounds):
    rows_query = query_block.shape[0]
    rows_key = key_window.shape[0]
    query_doc = positions_doc(query_pos, bounds)
    key_doc = positions_doc(key_pos, bounds)
    allowed = (
        (query_doc[:, None] == key_doc[None, :])
        & (key_pos[None, :] <= query_pos[:, None])
        & (key_pos[None, :] >= 0)
    )
    scale = 1.0 / math.sqrt(HD)
    grouped_query = query_block.reshape(rows_query, KVH, GROUP, HD).transpose(1, 2, 0, 3)
    grouped_grad = grad_block.reshape(rows_query, KVH, GROUP, HD).transpose(1, 2, 0, 3)
    keyed = key_window.reshape(rows_key, KVH, HD).transpose(1, 0, 2)
    valued = value_window.reshape(rows_key, KVH, HD).transpose(1, 0, 2)

    def per_head(operands):
        query_head, key_head, value_head, grad_head = operands
        scores = (
            jnp.einsum("gtd,sd->gts", query_head, key_head, preferred_element_type=jnp.float32)
            * scale
        )
        masked = jnp.where(allowed[None], scores, jnp.float32(-1e30))
        top_score = jnp.max(masked, axis=-1, keepdims=True)
        weights = jnp.where(allowed[None], jnp.exp(masked - top_score), jnp.float32(0.0))
        probs = weights / jnp.sum(weights, axis=-1, keepdims=True)
        probs_low = probs.astype(jnp.bfloat16)
        attn = jnp.einsum(
            "gts,sd->gtd", probs_low, value_head, preferred_element_type=jnp.float32
        ).astype(jnp.bfloat16)
        dprobs = jnp.einsum(
            "gtd,sd->gts", grad_head, value_head, preferred_element_type=jnp.float32
        )
        delta = jnp.sum(
            grad_head.astype(jnp.float32) * attn.astype(jnp.float32), axis=-1, keepdims=True
        )
        dscores = (probs * (dprobs - delta) * scale).astype(jnp.bfloat16)
        dquery = jnp.einsum("gts,sd->gtd", dscores, key_head, preferred_element_type=jnp.float32)
        dkey = jnp.einsum("gts,gtd->sd", dscores, query_head, preferred_element_type=jnp.float32)
        dvalue = jnp.einsum("gts,gtd->sd", probs_low, grad_head, preferred_element_type=jnp.float32)
        return (attn, dquery, dkey, dvalue)

    attn, dquery, dkey, dvalue = lax.map(per_head, (grouped_query, keyed, valued, grouped_grad))
    attn = attn.transpose(2, 0, 1, 3).reshape(rows_query, KVH * GROUP * HD)
    dquery = dquery.transpose(2, 0, 1, 3).reshape(rows_query, KVH * GROUP * HD)
    dkey = dkey.transpose(1, 0, 2).reshape(rows_key, KVH * HD)
    dvalue = dvalue.transpose(1, 0, 2).reshape(rows_key, KVH * HD)
    return (attn, dquery, dkey, dvalue)


def on_device(queries, key_rows, value_rows, grad_out, doc_lengths):
    query_local = queries[0]
    key_local = key_rows[0]
    value_local = value_rows[0]
    grad_local = grad_out[0]
    tok_rows = query_local.shape[0]
    kv_width = key_local.shape[1]
    position = lax.axis_index("ctx")
    bounds = jnp.cumsum(doc_lengths[0])
    current = (key_local, value_local)
    arrived = []
    for distance in range(1, DOC_SPAN + 1):
        current = passed_along((current[0], current[1]), "ctx", 1)
        arrived.append(current)
    earlier = arrived[::-1]
    key_window = jnp.concatenate([item[0] for item in earlier] + [key_local], axis=0)
    value_window = jnp.concatenate([item[1] for item in earlier] + [value_local], axis=0)
    query_pos = position * tok_rows + jnp.arange(tok_rows, dtype=jnp.int32)
    key_pos = (position - DOC_SPAN) * tok_rows + jnp.arange(
        (DOC_SPAN + 1) * tok_rows, dtype=jnp.int32
    )
    attn, dquery, dkey_window, dvalue_window = window_attention(
        query_local, key_window, value_window, grad_local, query_pos, key_pos, bounds
    )
    key_parts = dkey_window.reshape(DOC_SPAN + 1, tok_rows, kv_width)
    value_parts = dvalue_window.reshape(DOC_SPAN + 1, tok_rows, kv_width)
    carried = (key_parts[0], value_parts[0])
    for distance in range(DOC_SPAN - 1, -1, -1):
        moved = passed_along((carried[0], carried[1]), "ctx", -1)
        carried = (
            moved[0] + key_parts[DOC_SPAN - distance],
            moved[1] + value_parts[DOC_SPAN - distance],
        )
    dkey_full, dvalue_full = carried
    local_sums = jnp.concatenate(
        [jnp.sum(dquery, axis=0), jnp.sum(dkey_full, axis=0), jnp.sum(dvalue_full, axis=0)]
    )
    within = lax.psum(local_sums, "ctx")
    bias_grad = lax.psum(within, "dp")
    return (
        attn[None],
        dquery.astype(jnp.bfloat16)[None],
        dkey_full.astype(jnp.bfloat16)[None],
        dvalue_full.astype(jnp.bfloat16)[None],
        bias_grad,
    )


def solution(mesh):
    return jax.shard_map(
        on_device,
        mesh=mesh,
        in_specs=(
            P("dp", "ctx", None),
            P("dp", "ctx", None),
            P("dp", "ctx", None),
            P("dp", "ctx", None),
            P("dp", None),
        ),
        out_specs=(
            P("dp", "ctx", None),
            P("dp", "ctx", None),
            P("dp", "ctx", None),
            P("dp", "ctx", None),
            P(),
        ),
        check_vma=False,
    )
```

profile of v0, /device:TPU:32, one launch (start us, length us, event | category | flops | bytes accessed | tf_op | source)
XLA Modules:
  0.0 515.9 jit_solution(4158142984814327837)
XLA Ops:
  0.6 1.9 collective-permute-start.4
  3.6 3.5 collective-permute-start
  7.2 5.6 %collective-permute-done.4 = bf16[256,512]{1,0:T(8,128)(2,1)S(1)} collective-permute-done((bf16[256,512]{1,0:T(8,128)(2,1)}, bf16[256,512]{1,0:T(8,128)(2,1)S(1)}, u32[]{:S(2)}, u32[]{:S(2)}) %collective-permute-start.4) | collective-permute-done | bytes 262176 | tf_op jit(solution)/shard_map/ppermute | solution.py:17
  12.8 1.9 collective-permute-start.5
  15.6 1.9 collective-permute-start.1
  17.5 7.2 %collective-permute-done.5 = bf16[256,512]{1,0:T(8,128)(2,1)S(1)} collective-permute-done((bf16[256,512]{1,0:T(8,128)(2,1)S(1)}, bf16[256,512]{1,0:T(8,128)(2,1)S(1)}, u32[]{:S(2)}, u32[]{:S(2)}) %collective-permute-start.5) | collective-permute-done | bytes 262176 | tf_op jit(solution)/shard_map/ppermute | solution.py:17
  24.7 1.9 collective-permute-start.6
  27.5 1.9 collective-permute-start.2
  30.4 6.3 %collective-permute-done.6 = bf16[256,512]{1,0:T(8,128)(2,1)} collective-permute-done((bf16[256,512]{1,0:T(8,128)(2,1)S(1)}, bf16[256,512]{1,0:T(8,128)(2,1)}, u32[]{:S(2)}, u32[]{:S(2)}) %collective-permute-start.6) | collective-permute-done | bytes 262176 | tf_op jit(solution)/shard_map/ppermute | solution.py:17
  36.7 1.9 collective-permute-start.7
  39.5 1.9 collective-permute-start.3
  57.8 85.5 %while.17 = (s32[]{:T(128)}, bf16[4,5,256,128]{2,3,1,0:T(8,128)(2,1)}, f32[4,5,256,128]{2,3,1,0:T(8,128)}, f32[4,1280,128]{2,1,0:T(8,128)}, f32[4,1280,128]{2,1,...) while((s32[]{:T(128)}, ...), condition=%wide.region_7.8_spmd.clone, body=%wide.region_3.7_spmd.clone.sunk | while | flops 2538373120 | bytes 71158240 | solution.py:66
  58.2 6.7 %fusion.88 = (f32[5,256]{1,0:T(8,128)S(1)}, f32[5,256,1280]{2,1,0:T(8,128)}) fusion(pred[256,1280]{1,0:T(8,128)(4,1)S(1)} %and_and_fusion.2, bf16[4,1280,128]{1,2,0:T(8,128)(2,1)} %get-tuple-element.312, s32[]{:T(128)S(6)} %copy.154, bf16[4,5,256,128]{2,3,1,0:T(8,128)(2,1)S(1)} %get-tuple-element.311), kind=kOutput, calls=%fused_computation.94.clone.1 | convolution fusion | flops 427623680 | bytes 7870464 | tf_op jit(solution)/shard_map/while/body/eval_jaxpr/sub | solution.py:48
  64.9 3.7 fusion.89
  68.6 1.9 bitcast_dynamic-update-slice_fusion.2
  70.5 1.9 fusion.92
  74.2 1.9 fusion.91
  76.1 3.0 fusion.90
  79.5 6.7 %fusion.88 = (f32[5,256]{1,0:T(8,128)S(1)}, f32[5,256,1280]{2,1,0:T(8,128)}) fusion(pred[256,1280]{1,0:T(8,128)(4,1)S(1)} %and_and_fusion.2, bf16[4,1280,128]{1,2,0:T(8,128)(2,1)} %get-tuple-element.312, s32[]{:T(128)S(6)} %copy.154, bf16[4,5,256,128]{2,3,1,0:T(8,128)(2,1)S(1)} %get-tuple-element.311), kind=kOutput, calls=%fused_computation.94.clone.1 | convolution fusion | flops 427623680 | bytes 7870464 | tf_op jit(solution)/shard_map/while/body/eval_jaxpr/sub | solution.py:48
  86.2 3.7 fusion.89
  89.9 1.9 bitcast_dynamic-update-slice_fusion.2
  91.9 1.9 fusion.92
  97.5 3.0 fusion.90
  100.8 6.7 %fusion.88 = (f32[5,256]{1,0:T(8,128)S(1)}, f32[5,256,1280]{2,1,0:T(8,128)}) fusion(pred[256,1280]{1,0:T(8,128)(4,1)S(1)} %and_and_fusion.2, bf16[4,1280,128]{1,2,0:T(8,128)(2,1)} %get-tuple-element.312, s32[]{:T(128)S(6)} %copy.154, bf16[4,5,256,128]{2,3,1,0:T(8,128)(2,1)S(1)} %get-tuple-element.311), kind=kOutput, calls=%fused_computation.94.clone.1 | convolution fusion | flops 427623680 | bytes 7870464 | tf_op jit(solution)/shard_map/while/body/eval_jaxpr/sub | solution.py:48
  107.5 3.7 fusion.89
  111.2 1.9 bitcast_dynamic-update-slice_fusion.2
  113.2 2.0 fusion.92
  116.9 1.9 fusion.91
  118.8 3.1 fusion.90
  122.3 6.7 %fusion.88 = (f32[5,256]{1,0:T(8,128)S(1)}, f32[5,256,1280]{2,1,0:T(8,128)}) fusion(pred[256,1280]{1,0:T(8,128)(4,1)S(1)} %and_and_fusion.2, bf16[4,1280,128]{1,2,0:T(8,128)(2,1)} %get-tuple-element.312, s32[]{:T(128)S(6)} %copy.154, bf16[4,5,256,128]{2,3,1,0:T(8,128)(2,1)S(1)} %get-tuple-element.311), kind=kOutput, calls=%fused_computation.94.clone.1 | convolution fusion | flops 427623680 | bytes 7870464 | tf_op jit(solution)/shard_map/while/body/eval_jaxpr/sub | solution.py:48
  129.0 3.7 fusion.89
  132.7 1.9 bitcast_dynamic-update-slice_fusion.2
  134.6 1.9 fusion.92
  140.2 3.1 fusion.90
  143.3 2.0 slice_bitcast_fusion
  145.3 7.9 %collective-permute-start.12 = (f32[256,512]{1,0:T(8,128)S(1)}, f32[256,512]{1,0:T(8,128)S(1)}, u32[]{:S(2)}, u32[]{:S(2)}) collective-permute-start(f32[256,512]{1,0:T(8,128)S(1)} %bitcast.199), channel_id=1, source_target_pairs={{1,0},{2,1},{3,2},{4,3},{5,4},{6,5},{7,6},{8,7},{9,8},{10,9},{11,1... | collective-permute-start | bytes 1572872 | tf_op jit(solution)/shard_map/ppermute | solution.py:17
  154.3 1.9 collective-permute-start.8
  156.2 3.6 collective-permute-done.12
  160.0 8.0 %collective-permute-start.13 = (f32[256,512]{1,0:T(8,128)S(1)}, f32[256,512]{1,0:T(8,128)S(1)}, u32[]{:S(2)}, u32[]{:S(2)}) collective-permute-start(f32[256,512]{1,0:T(8,128)S(1)} %bitcast_add_fusion.3), channel_id=1, source_target_pairs={{1,0},{2,1},{3,2},{4,3},{5,4},{6,5},{7,6},{8,7},{9,8},{10,9},{11,1... | collective-permute-start | bytes 1572872 | tf_op jit(solution)/shard_map/ppermute | solution.py:17
  168.1 5.5 %collective-permute-start.9 = (f32[256,512]{1,0:T(8,128)S(1)}, f32[256,512]{1,0:T(8,128)S(1)}, u32[]{:S(2)}, u32[]{:S(2)}) collective-permute-start(f32[256,512]{1,0:T(8,128)S(1)} %bitcast_add_fusion.7), channel_id=1, source_target_pairs={{1,0},{2,1},{3,2},{4,3},{5,4},{6,5},{7,6},{8,7},{9,8},{10,9},{11,1... | collective-permute-start | bytes 1572872 | tf_op jit(solution)/shard_map/ppermute | solution.py:17
  174.7 8.0 %collective-permute-start.14 = (f32[256,512]{1,0:T(8,128)S(1)}, f32[256,512]{1,0:T(8,128)S(1)}, u32[]{:S(2)}, u32[]{:S(2)}) collective-permute-start(f32[256,512]{1,0:T(8,128)S(1)} %bitcast_add_fusion.2), channel_id=1, source_target_pairs={{1,0},{2,1},{3,2},{4,3},{5,4},{6,5},{7,6},{8,7},{9,8},{10,9},{11,1... | collective-permute-start | bytes 1572872 | tf_op jit(solution)/shard_map/ppermute | solution.py:17
  182.9 5.5 %collective-permute-start.10 = (f32[256,512]{1,0:T(8,128)S(1)}, f32[256,512]{1,0:T(8,128)S(1)}, u32[]{:S(2)}, u32[]{:S(2)}) collective-permute-start(f32[256,512]{1,0:T(8,128)S(1)} %bitcast_add_fusion.6), channel_id=1, source_target_pairs={{1,0},{2,1},{3,2},{4,3},{5,4},{6,5},{7,6},{8,7},{9,8},{10,9},{11,1... | collective-permute-start | bytes 1572872 | tf_op jit(solution)/shard_map/ppermute | solution.py:17
  190.3 8.2 %collective-permute-start.15 = (f32[256,512]{1,0:T(8,128)}, f32[256,512]{1,0:T(8,128)}, u32[]{:S(2)}, u32[]{:S(2)}) collective-permute-start(f32[256,512]{1,0:T(8,128)} %bitcast_add_fusion.1), channel_id=1, source_target_pairs={{1,0},{2,1},{3,2},{4,3},{5,4},{6,5},{7,6},{8,7},{9,8},{10,9},{11,1... | collective-permute-start | bytes 1572872 | tf_op jit(solution)/shard_map/ppermute | solution.py:17
  199.4 4.6 collective-permute-start.11
  204.4 2.4 copy.92
  208.1 2.4 copy.93
  214.3 279.7 %psum.14 = f32[3584]{0:T(1024)S(1)} all-reduce(f32[3584]{0:T(1024)S(1)} %pad_maximum_fusion), channel_id=1, replica_groups=mesh['dp'=4,'ctx'=64] {'ctx'}, use_global_device_ids=true, to_apply=%region_11.12 | all-reduce | flops 3584 | bytes 28672 | tf_op jit(solution)/shard_map/psum | solution.py:111
  494.0 21.9 %psum.15 = f32[3584]{0:T(1024)} all-reduce(f32[3584]{0:T(1024)S(1)} %psum.14), channel_id=1, replica_groups=mesh['dp'=4,'ctx'=64] {'dp'}, use_global_device_ids=true, to_apply=%region_12.13 | all-reduce | flops 3584 | bytes 28672 | tf_op jit(solution)/shard_map/psum | solution.py:112
  (123 shorter events, 43.9 us)
Async XLA Ops:
  0.6 12.1 %collective-permute-start.4 = (bf16[256,512]{1,0:T(8,128)(2,1)}, bf16[256,512]{1,0:T(8,128)(2,1)S(1)}, u32[]{:S(2)}, u32[]{:S(2)}) collective-permute-start(bf16[256,512]{1,0:T(8,128)(2,1)} %bitcast.201), channel_id=1, source_target_pairs={{0,1},{1,2},{2,3},{3,4},{4,5},{5,6},{6,7},{7,8},{8,9},{9,10},{10,1... | collective-permute-start | bytes 786440 | tf_op jit(solution)/shard_map/ppermute | solution.py:17
  3.6 11.9 %collective-permute-start = (bf16[256,512]{0,1:T(8,128)(2,1)S(1)}, bf16[256,512]{0,1:T(8,128)(2,1)S(1)}, u32[]{:S(2)}, u32[]{:S(2)}) collective-permute-start(bf16[256,512]{0,1:T(8,128)(2,1)S(1)} %bitcast.192), channel_id=1, source_target_pairs={{0,1},{1,2},{2,3},{3,4},{4,5},{5,6},{6,7},{7,8},{8,9},{9,10},{10,1... | collective-permute-start | bytes 786440 | tf_op jit(solution)/shard_map/ppermute | solution.py:17
  12.8 29.8 %copy-start.11 = (bf16[256,512]{1,0:T(8,128)(2,1)}, bf16[256,512]{1,0:T(8,128)(2,1)S(1)}, u32[]{:S(2)}) copy-start(bf16[256,512]{1,0:T(8,128)(2,1)S(1)} %collective-permute-done.4) | copy-start | bytes 786436
  12.8 11.9 %collective-permute-start.5 = (bf16[256,512]{1,0:T(8,128)(2,1)S(1)}, bf16[256,512]{1,0:T(8,128)(2,1)S(1)}, u32[]{:S(2)}, u32[]{:S(2)}) collective-permute-start(bf16[256,512]{1,0:T(8,128)(2,1)S(1)} %collective-permute-done.4), channel_id=1, source_target_pairs={{0,1},{1,2},{2,3},{3,4},{4,5},{5,6},{6,7},{7,8},{8,9},{9,10},{10,1... | collective-permute-start | bytes 786440 | tf_op jit(solution)/shard_map/ppermute | solution.py:17
  15.6 27.0 %copy-start.7 = (bf16[256,512]{0,1:T(8,128)(2,1)}, bf16[256,512]{0,1:T(8,128)(2,1)S(1)}, u32[]{:S(2)}) copy-start(bf16[256,512]{0,1:T(8,128)(2,1)S(1)} %collective-permute-done) | copy-start | bytes 786436
  15.6 11.9 %collective-permute-start.1 = (bf16[256,512]{0,1:T(8,128)(2,1)S(1)}, bf16[256,512]{0,1:T(8,128)(2,1)S(1)}, u32[]{:S(2)}, u32[]{:S(2)}) collective-permute-start(bf16[256,512]{0,1:T(8,128)(2,1)S(1)} %collective-permute-done), channel_id=1, source_target_pairs={{0,1},{1,2},{2,3},{3,4},{4,5},{5,6},{6,7},{7,8},{8,9},{9,10},{10,1... | collective-permute-start | bytes 786440 | tf_op jit(solution)/shard_map/ppermute | solution.py:17
  24.7 17.9 %copy-start.12 = (bf16[256,512]{1,0:T(8,128)(2,1)}, bf16[256,512]{1,0:T(8,128)(2,1)S(1)}, u32[]{:S(2)}) copy-start(bf16[256,512]{1,0:T(8,128)(2,1)S(1)} %collective-permute-done.5) | copy-start | bytes 786436
  24.7 12.0 %collective-permute-start.6 = (bf16[256,512]{1,0:T(8,128)(2,1)S(1)}, bf16[256,512]{1,0:T(8,128)(2,1)}, u32[]{:S(2)}, u32[]{:S(2)}) collective-permute-start(bf16[256,512]{1,0:T(8,128)(2,1)S(1)} %collective-permute-done.5), channel_id=1, source_target_pairs={{0,1},{1,2},{2,3},{3,4},{4,5},{5,6},{6,7},{7,8},{8,9},{9,10},{10,1... | collective-permute-start | bytes 786440 | tf_op jit(solution)/shard_map/ppermute | solution.py:17
  27.5 13.9 %copy-start.9 = (bf16[256,512]{0,1:T(8,128)(2,1)}, bf16[256,512]{0,1:T(8,128)(2,1)S(1)}, u32[]{:S(2)}) copy-start(bf16[256,512]{0,1:T(8,128)(2,1)S(1)} %collective-permute-done.1) | copy-start | bytes 786436
  27.5 12.0 %collective-permute-start.2 = (bf16[256,512]{0,1:T(8,128)(2,1)S(1)}, bf16[256,512]{0,1:T(8,128)(2,1)}, u32[]{:S(2)}, u32[]{:S(2)}) collective-permute-start(bf16[256,512]{0,1:T(8,128)(2,1)S(1)} %collective-permute-done.1), channel_id=1, source_target_pairs={{0,1},{1,2},{2,3},{3,4},{4,5},{5,6},{6,7},{7,8},{8,9},{9,10},{10,1... | collective-permute-start | bytes 786440 | tf_op jit(solution)/shard_map/ppermute | solution.py:17
  36.7 13.9 %collective-permute-start.7 = (bf16[256,512]{1,0:T(8,128)(2,1)}, bf16[256,512]{1,0:T(8,128)(2,1)}, u32[]{:S(2)}, u32[]{:S(2)}) collective-permute-start(bf16[256,512]{1,0:T(8,128)(2,1)} %collective-permute-done.6), channel_id=1, source_target_pairs={{0,1},{1,2},{2,3},{3,4},{4,5},{5,6},{6,7},{7,8},{8,9},{9,10},{10,1... | collective-permute-start | bytes 786440 | tf_op jit(solution)/shard_map/ppermute | solution.py:17
  39.5 13.9 %collective-permute-start.3 = (bf16[256,512]{0,1:T(8,128)(2,1)}, bf16[256,512]{0,1:T(8,128)(2,1)}, u32[]{:S(2)}, u32[]{:S(2)}) collective-permute-start(bf16[256,512]{0,1:T(8,128)(2,1)} %collective-permute-done.2), channel_id=1, source_target_pairs={{0,1},{1,2},{2,3},{3,4},{4,5},{5,6},{6,7},{7,8},{8,9},{9,10},{10,1... | collective-permute-start | bytes 786440 | tf_op jit(solution)/shard_map/ppermute | solution.py:17
  52.4 3.0 copy-start.6
  54.4 2.3 copy-start.10
  55.4 1.3 copy-start.8
  55.5 1.3 copy-start.2
  56.8 1.1 copy-start.1
  64.9 3.7 copy-start.3
  64.9 7.7 %slice-start = ((s8[6553600]{0:T(1024)(128)(4,1)}), s8[4194304]{0:T(1024)(128)(4,1)S(1)}, s32[]{:S(2)}) async-start(s8[6553600]{0:T(1024)(128)(4,1)} %bitcast.182), calls=%async_computation | async-start | bytes 8388608 | tf_op jit(solution)/shard_map/while
  68.6 4.0 slice-start.1
  86.2 3.7 copy-start.3
  86.2 7.7 %slice-start = ((s8[6553600]{0:T(1024)(128)(4,1)}), s8[4194304]{0:T(1024)(128)(4,1)S(1)}, s32[]{:S(2)}) async-start(s8[6553600]{0:T(1024)(128)(4,1)} %bitcast.182), calls=%async_computation | async-start | bytes 8388608 | tf_op jit(solution)/shard_map/while
  89.9 4.0 slice-start.1
  107.5 3.7 copy-start.3
  107.5 7.7 %slice-start = ((s8[6553600]{0:T(1024)(128)(4,1)}), s8[4194304]{0:T(1024)(128)(4,1)S(1)}, s32[]{:S(2)}) async-start(s8[6553600]{0:T(1024)(128)(4,1)} %bitcast.182), calls=%async_computation | async-start | bytes 8388608 | tf_op jit(solution)/shard_map/while
  111.2 4.0 slice-start.1
  129.0 3.7 copy-start.3
  129.0 7.7 %slice-start = ((s8[6553600]{0:T(1024)(128)(4,1)}), s8[4194304]{0:T(1024)(128)(4,1)S(1)}, s32[]{:S(2)}) async-start(s8[6553600]{0:T(1024)(128)(4,1)} %bitcast.182), calls=%async_computation | async-start | bytes 8388608 | tf_op jit(solution)/shard_map/while
  132.7 4.0 slice-start.1
  143.3 9.9 %copy-start.4 = (f32[4,1280,128]{2,1,0:T(8,128)S(1)}, f32[4,1280,128]{2,1,0:T(8,128)}, u32[]{:S(2)}) copy-start(f32[4,1280,128]{2,1,0:T(8,128)} %get-tuple-element.62) | copy-start | bytes 7864324
  145.3 14.5 %collective-permute-start.12 = (f32[256,512]{1,0:T(8,128)S(1)}, f32[256,512]{1,0:T(8,128)S(1)}, u32[]{:S(2)}, u32[]{:S(2)}) collective-permute-start(f32[256,512]{1,0:T(8,128)S(1)} %bitcast.199), channel_id=1, source_target_pairs={{1,0},{2,1},{3,2},{4,3},{5,4},{6,5},{7,6},{8,7},{9,8},{10,9},{11,1... | collective-permute-start | bytes 1572872 | tf_op jit(solution)/shard_map/ppermute | solution.py:17
  154.3 13.7 %collective-permute-start.8 = (f32[256,512]{1,0:T(8,128)S(1)}, f32[256,512]{1,0:T(8,128)S(1)}, u32[]{:S(2)}, u32[]{:S(2)}) collective-permute-start(f32[256,512]{1,0:T(8,128)S(1)} %bitcast.200), channel_id=1, source_target_pairs={{1,0},{2,1},{3,2},{4,3},{5,4},{6,5},{7,6},{8,7},{9,8},{10,9},{11,1... | collective-permute-start | bytes 1572872 | tf_op jit(solution)/shard_map/ppermute | solution.py:17
  160.0 14.7 %collective-permute-start.13 = (f32[256,512]{1,0:T(8,128)S(1)}, f32[256,512]{1,0:T(8,128)S(1)}, u32[]{:S(2)}, u32[]{:S(2)}) collective-permute-start(f32[256,512]{1,0:T(8,128)S(1)} %bitcast_add_fusion.3), channel_id=1, source_target_pairs={{1,0},{2,1},{3,2},{4,3},{5,4},{6,5},{7,6},{8,7},{9,8},{10,9},{11,1... | collective-permute-start | bytes 1572872 | tf_op jit(solution)/shard_map/ppermute | solution.py:17
  168.1 14.7 %collective-permute-start.9 = (f32[256,512]{1,0:T(8,128)S(1)}, f32[256,512]{1,0:T(8,128)S(1)}, u32[]{:S(2)}, u32[]{:S(2)}) collective-permute-start(f32[256,512]{1,0:T(8,128)S(1)} %bitcast_add_fusion.7), channel_id=1, source_target_pairs={{1,0},{2,1},{3,2},{4,3},{5,4},{6,5},{7,6},{8,7},{9,8},{10,9},{11,1... | collective-permute-start | bytes 1572872 | tf_op jit(solution)/shard_map/ppermute | solution.py:17
  174.7 14.7 %collective-permute-start.14 = (f32[256,512]{1,0:T(8,128)S(1)}, f32[256,512]{1,0:T(8,128)S(1)}, u32[]{:S(2)}, u32[]{:S(2)}) collective-permute-start(f32[256,512]{1,0:T(8,128)S(1)} %bitcast_add_fusion.2), channel_id=1, source_target_pairs={{1,0},{2,1},{3,2},{4,3},{5,4},{6,5},{7,6},{8,7},{9,8},{10,9},{11,1... | collective-permute-start | bytes 1572872 | tf_op jit(solution)/shard_map/ppermute | solution.py:17
  182.9 15.6 %collective-permute-start.10 = (f32[256,512]{1,0:T(8,128)S(1)}, f32[256,512]{1,0:T(8,128)S(1)}, u32[]{:S(2)}, u32[]{:S(2)}) collective-permute-start(f32[256,512]{1,0:T(8,128)S(1)} %bitcast_add_fusion.6), channel_id=1, source_target_pairs={{1,0},{2,1},{3,2},{4,3},{5,4},{6,5},{7,6},{8,7},{9,8},{10,9},{11,1... | collective-permute-start | bytes 1572872 | tf_op jit(solution)/shard_map/ppermute | solution.py:17
  189.5 14.5 %copy-start = (f32[4,5,256,128]{2,3,1,0:T(8,128)S(1)}, f32[4,5,256,128]{2,3,1,0:T(8,128)}, u32[]{:S(2)}) copy-start(f32[4,5,256,128]{2,3,1,0:T(8,128)} %get-tuple-element.61) | copy-start | bytes 7864324
  190.3 20.2 %collective-permute-start.15 = (f32[256,512]{1,0:T(8,128)}, f32[256,512]{1,0:T(8,128)}, u32[]{:S(2)}, u32[]{:S(2)}) collective-permute-start(f32[256,512]{1,0:T(8,128)} %bitcast_add_fusion.1), channel_id=1, source_target_pairs={{1,0},{2,1},{3,2},{4,3},{5,4},{6,5},{7,6},{8,7},{9,8},{10,9},{11,1... | collective-permute-start | bytes 1572872 | tf_op jit(solution)/shard_map/ppermute | solution.py:17
  199.4 13.0 %collective-permute-start.11 = (f32[256,512]{1,0:T(8,128)}, f32[256,512]{1,0:T(8,128)}, u32[]{:S(2)}, u32[]{:S(2)}) collective-permute-start(f32[256,512]{1,0:T(8,128)} %bitcast_add_fusion.5), channel_id=1, source_target_pairs={{1,0},{2,1},{3,2},{4,3},{5,4},{6,5},{7,6},{8,7},{9,8},{10,9},{11,1... | collective-permute-start | bytes 1572872 | tf_op jit(solution)/shard_map/ppermute | solution.py:17
  210.5 1.9 copy-start.5
where the time goes:
time: 517 us; the launch traced here: 516 us
  blocking collectives  302 us (58%)
  matrix products  68.4 us (13%)
  starting transfers between devices  66.6 us (13%)
  waiting for transfers between devices  27.4 us (5%)
  local copies, waits for them, and re-layouts  25.9 us (5%)
  other arithmetic  24.5 us (5%)
    psum x1, blocking collectives, on_device(): within = lax.psum(local_sums, 'ctx')  280 us
    ppermute x16, starting transfers between devices, passed_along(): return lax.ppermute(shard, axis, pairs)  66.6 us
    ppermute x16, waiting for transfers between devices, passed_along(): return lax.ppermute(shard, axis, pairs)  27.4 us
    sub x4, matrix products, per_head(): masked - top_score  26.7 us
    psum x1, blocking collectives, on_device(): bias_grad = lax.psum(within, 'dp')  21.9 us
    unnamed x40, local copies, waits for them, and re-layouts  18.5 us
    convert_element_type x4, other arithmetic, per_head(): probs_low = probs.astype(jnp.bfloat16)  14.8 us
    dot_general x4, matrix products, per_head(): jnp.einsum('gts,sd->gtd', dscores, key_head, preferred_element_type=jnp.f...  12.1 us
  transfers between devices with their start and end apart: 16, of which 9 were waited for; matrix products, arithmetic and copies ran while one was open for 5% of the time, Pallas kernels for 0%

commit v1 on v0

v1 whole, which is shorter than its diff:
```python
import math

import jax
import jax.numpy as jnp
from jax import lax
from jax.experimental import pallas as pl
from jax.experimental.pallas import tpu as pltpu
from jax.sharding import PartitionSpec as P

KVH = 4
HD = 128
GROUP = 5
TOK = 256
SPAN = 4
WIN = (SPAN + 1) * TOK
HALF = 128
HWIN = SPAN * TOK + HALF
GW = GROUP * HD
DOCS = 32
SCALE = 1.0 / math.sqrt(HD)
SCALE2 = SCALE * math.log2(math.e)
NT = (((1,), (1,)), ((), ()))
MESH = pl.DeviceIdType.MESH
F32 = jnp.float32
BF16 = jnp.bfloat16
COMPUTE = True


def kernel(
    lens, q_hbm, k_hbm, v_hbm, do_hbm,
    o_hbm, dq_hbm, dk_hbm, dv_hbm, bias_out,
    q, do, ob, dqb, kv, part, stage, got, okv, mask, dkt, dvt,
    sums, b1, b2, b3,
    load_sem, kv_sem, out_sem, okv_sem,
    fs, fr, rs, rr, bs, br1, br2, br3,
):
    dp = lax.axis_index("dp")
    me = lax.axis_index("ctx")
    n = 64
    core = lax.rem(me, 2)
    nxt = lax.rem(me + 2, n)
    prv = lax.rem(me + n - 2, n)
    mate = me + 1 - 2 * core
    rank1 = lax.rem(me, 8)
    rank2 = lax.rem(me // 8, 4)
    zlo = me // 32
    rank3 = dp * 2 + zlo

    def peer1(d):
        return (dp, me - rank1 + lax.rem(rank1 + d, 8))

    def peer2(d):
        return (dp, me + 8 * (lax.rem(rank2 + d, 4) - rank2))

    def peer3(d):
        r = lax.rem(rank3 + d, 8)
        return (r // 2, me + 32 * (lax.rem(r, 2) - zlo))

    def kvload(g):
        c = g * HD
        return (
            pltpu.make_async_copy(k_hbm.at[0, :, pl.ds(c, HD)], kv.at[g, 0, pl.ds(SPAN * TOK, TOK)], kv_sem.at[g, 0]),
            pltpu.make_async_copy(v_hbm.at[0, :, pl.ds(c, HD)], kv.at[g, 1, pl.ds(SPAN * TOK, TOK)], kv_sem.at[g, 1]),
        )

    def qload(g):
        c = pl.ds(pl.multiple_of(g * GW, 128), GW)
        return (
            pltpu.make_async_copy(q_hbm.at[0, :, c], q.at[:, c], load_sem.at[g, 0]),
            pltpu.make_async_copy(do_hbm.at[0, :, c], do.at[:, c], load_sem.at[g, 1]),
        )

    def ostore(g):
        c = pl.ds(pl.multiple_of(g * GW, 128), GW)
        return (
            pltpu.make_async_copy(ob.at[:, c], o_hbm.at[0, :, c], out_sem.at[g, 0]),
            pltpu.make_async_copy(dqb.at[:, c], dq_hbm.at[0, :, c], out_sem.at[g, 1]),
        )

    def fwd(kind, g, src_slot, dst_slot, to):
        return pltpu.make_async_remote_copy(
            src_ref=kv.at[g, :, pl.ds(src_slot * TOK, TOK)],
            dst_ref=kv.at[g, :, pl.ds(dst_slot * TOK, TOK)],
            send_sem=fs.at[g, kind],
            recv_sem=fr.at[g, kind],
            device_id=(dp, to),
            device_id_type=MESH,
        )

    def h1(g):
        return fwd(0, g, 4, 2, nxt)

    def h2(g):
        return fwd(1, g, 2, 0, nxt)

    def l1(g):
        return fwd(2, g, 4, 3, mate)

    def l2_from0(g):
        return fwd(3, g, 2, 1, mate)

    def l2_from1(g):
        return fwd(3, g, 2, 3, mate)

    def l3(g):
        return fwd(4, g, 0, 1, mate)

    def relay1(g):
        h1(g).wait_recv()
        h2(g).start()

        @pl.when(core == 0)
        def _():
            l2_from0(g).start()

        @pl.when(core == 1)
        def _():
            l2_from1(g).start()

    def relay2(g):
        h2(g).wait_recv()

        @pl.when(core == 1)
        def _():
            l3(g).start()

    def complete(g):
        @pl.when(core == 0)
        def _():
            l2_from1(g).wait_recv()
            l3(g).wait_recv()

        @pl.when(core == 1)
        def _():
            l1(g).wait_recv()
            l2_from0(g).wait_recv()

    def begin(g):
        h1(g).start()

        @pl.when(core == 0)
        def _():
            l1(g).start()

    def ret(kind, g, to):
        return pltpu.make_async_remote_copy(
            src_ref=stage.at[g, kind],
            dst_ref=got.at[g, kind],
            send_sem=rs.at[g, kind],
            recv_sem=rr.at[g, kind],
            device_id=(dp, to),
            device_id_type=MESH,
        )

    def r1(g):
        for kind, slot in ((0, 1), (1, 3)):
            for t in range(2):
                stage[g, kind, t] = part[g, t, slot * TOK:(slot + 1) * TOK].astype(BF16)
            ret(kind, g, mate).start()

    def r2(g):
        ret(0, g, mate).wait_recv()

        @pl.when(core == 0)
        def _():
            for t in range(2):
                stage[g, 2, t] = part[g, t, 0:TOK].astype(BF16)

        @pl.when(core == 1)
        def _():
            for t in range(2):
                stage[g, 2, t] = (part[g, t, 0:TOK] + got[g, 0, t].astype(F32)).astype(BF16)

        ret(2, g, prv).start()

    def r3(g):
        ret(1, g, mate).wait_recv()
        ret(2, g, prv).wait_recv()
        mine = slice(2 * TOK, 3 * TOK)

        @pl.when(core == 0)
        def _():
            for t in range(2):
                stage[g, 3, t] = (part[g, t, mine] + got[g, 0, t].astype(F32) + got[g, 2, t].astype(F32)).astype(BF16)

        @pl.when(core == 1)
        def _():
            for t in range(2):
                stage[g, 3, t] = (part[g, t, mine] + got[g, 1, t].astype(F32) + got[g, 2, t].astype(F32)).astype(BF16)

        ret(3, g, prv).start()

    def okv_store(g):
        c = pl.ds(pl.multiple_of(g * HD, 128), HD)
        return (
            pltpu.make_async_copy(okv.at[g, 0], dk_hbm.at[0, :, c], okv_sem.at[g, 0]),
            pltpu.make_async_copy(okv.at[g, 1], dv_hbm.at[0, :, c], okv_sem.at[g, 1]),
        )

    def r4(g):
        ret(3, g, prv).wait_recv()
        mine = slice(4 * TOK, 5 * TOK)

        @pl.when(core == 0)
        def _():
            for t in range(2):
                okv[g, t] = (part[g, t, mine] + got[g, 1, t].astype(F32) + got[g, 3, t].astype(F32)).astype(BF16)

        @pl.when(core == 1)
        def _():
            for t in range(2):
                okv[g, t] = (part[g, t, mine] + got[g, 3, t].astype(F32)).astype(BF16)

        for c in okv_store(g):
            c.start()

    def bias_send(buf, rank, peer, size, sem_at, recv):
        for d in range(1, size):
            pltpu.make_async_remote_copy(
                src_ref=buf.at[rank],
                dst_ref=buf.at[rank],
                send_sem=bs.at[sem_at + d],
                recv_sem=recv.at[rank],
                device_id=peer(d),
                device_id_type=MESH,
            ).start()

    def bias_wait(buf, rank, peer, size, sem_at, recv):
        for d in range(1, size):
            other = lax.rem(rank + d, size)
            pltpu.make_async_remote_copy(
                src_ref=buf.at[rank],
                dst_ref=buf.at[other],
                send_sem=bs.at[sem_at + d],
                recv_sem=recv.at[other],
                device_id=peer(d),
                device_id_type=MESH,
            ).wait()
        total = buf[0]
        for r in range(1, size):
            total = total + buf[r]
        return total

    for g in range(KVH):
        for c in kvload(g):
            c.start()
    for g in range(KVH):
        for c in qload(g):
            c.start()

    barrier = pltpu.get_barrier_semaphore()
    peers = [(dp, nxt), (dp, prv)]
    peers += [peer1(d) for d in range(1, 8)]
    peers += [peer2(d) for d in range(1, 4)]
    peers += [peer3(d) for d in range(1, 8)]
    for p in peers:
        pl.semaphore_signal(barrier, inc=1, device_id=p, device_id_type=MESH)
    pl.semaphore_wait(barrier, len(peers))

    for g in range(2):
        for c in kvload(g):
            c.wait()
        begin(g)

    where = me * TOK
    t_pos = lax.broadcasted_iota(jnp.int32, (TOK, 128), 0) + where
    first = jnp.zeros((TOK, 128), jnp.int32)
    bound = jnp.int32(0)
    for i in range(DOCS):
        bound = bound + lens[0, i]
        first = jnp.where(t_pos >= bound, bound, first)
    for c in range(WIN // 128):
        s_pos = lax.broadcasted_iota(jnp.int32, (TOK, 128), 1) + (where - SPAN * TOK + c * 128)
        mask[:, c * 128:(c + 1) * 128] = jnp.where((s_pos >= first) & (s_pos <= t_pos), 0.0, -1e30).astype(F32)

    for c in kvload(2):
        c.wait()
    relay1(0)
    begin(2)
    for c in kvload(3):
        c.wait()
    relay1(1)
    relay2(0)

    def unit(g, h):
        w0 = h * HALF
        rows = slice(w0, w0 + HALF)
        K = kv[g, 0, w0:w0 + HWIN]
        V = kv[g, 1, w0:w0 + HWIN]
        cols = [pl.ds(pl.multiple_of(g * GW + j * HD, 128), HD) for j in range(GROUP)]
        Q = jnp.concatenate([q[rows, c] for c in cols], 0)
        D = jnp.concatenate([do[rows, c] for c in cols], 0)
        bias = jnp.concatenate([mask[rows, w0:w0 + HWIN]] * GROUP, 0)
        s = lax.dot_general(Q, K, NT, preferred_element_type=F32) * SCALE2 + bias
        dprobs = lax.dot_general(D, V, NT, preferred_element_type=F32)
        m = jnp.max(s, axis=1, keepdims=True)
        w = jnp.exp2(s - m)
        inv = 1.0 / jnp.sum(w, axis=1, keepdims=True)
        low = (w * inv).astype(BF16)
        o = jnp.dot(low, V, preferred_element_type=F32).astype(BF16)
        delta = jnp.sum(D.astype(F32) * o.astype(F32), axis=1, keepdims=True)
        ds = ((w * (inv * SCALE)) * (dprobs - delta)).astype(BF16)
        dq = jnp.dot(ds, K, preferred_element_type=F32)
        for j, c in enumerate(cols):
            ob[rows, c] = o[j * HALF:(j + 1) * HALF]
            dqj = dq[j * HALF:(j + 1) * HALF]
            dqb[rows, c] = dqj.astype(BF16)
            dqs = jnp.sum(dqj, axis=0, keepdims=True)
            if h == 0:
                sums[g, j:j + 1] = dqs
            else:
                sums[g, j:j + 1] += dqs
        a1 = jnp.dot(Q.T, ds, preferred_element_type=F32)
        a2 = jnp.dot(D.T, low, preferred_element_type=F32)
        if h == 0:
            dkt[:, :HWIN] = a1
            dvt[:, :HWIN] = a2
            dkt[:, HWIN:] = jnp.zeros((HD, WIN - HWIN), F32)
            dvt[:, HWIN:] = jnp.zeros((HD, WIN - HWIN), F32)
        else:
            dkt[:, w0:] += a1
            dvt[:, w0:] += a2

    def finish(g):
        dk = dkt[...].T
        dv = dvt[...].T
        part[g, 0] = dk
        part[g, 1] = dv
        sums[g, 5:6] = jnp.sum(dk, axis=0, keepdims=True)
        sums[g, 6:7] = jnp.sum(dv, axis=0, keepdims=True)
        sums[g, 7:8] = jnp.zeros((1, HD), F32)

    def body(g, carry):
        complete(g)
        for c in qload(g):
            c.wait()
        if COMPUTE:
            unit(g, 0)

        @pl.when(g < 3)
        def _():
            relay2(g + 1)

        @pl.when(g < 2)
        def _():
            relay1(g + 2)

        @pl.when(g < 1)
        def _():
            begin(g + 3)

        @pl.when(g > 0)
        def _():
            r2(g - 1)

        @pl.when(g > 1)
        def _():
            r4(g - 2)

        if COMPUTE:
            unit(g, 1)
            finish(g)
        r1(g)
        for c in ostore(g):
            c.start()

        @pl.when(g > 0)
        def _():
            r3(g - 1)

        return carry

    lax.fori_loop(0, KVH, body, 0)

    b1[rank1] = sums[...]
    bias_send(b1, rank1, peer1, 8, 0, br1)
    r2(3)
    total = bias_wait(b1, rank1, peer1, 8, 0, br1)
    b2[rank2] = total
    bias_send(b2, rank2, peer2, 4, 8, br2)
    r4(2)
    r3(3)
    total = bias_wait(b2, rank2, peer2, 4, 8, br2)
    b3[rank3] = total
    bias_send(b3, rank3, peer3, 8, 12, br3)
    total = bias_wait(b3, rank3, peer3, 8, 12, br3)
    for g in range(KVH):
        bias_out[g * GROUP:(g + 1) * GROUP] = total[g, 0:GROUP]
        bias_out[20 + g:21 + g] = total[g, 5:6]
        bias_out[24 + g:25 + g] = total[g, 6:7]
    r4(3)

    def drain(g, carry):
        h1(g).wait_send()
        h2(g).wait_send()

        @pl.when(core == 0)
        def _():
            l1(g).wait_send()
            l2_from0(g).wait_send()

        @pl.when(core == 1)
        def _():
            l2_from1(g).wait_send()
            l3(g).wait_send()

        ret(0, g, mate).wait_send()
        ret(1, g, mate).wait_send()
        ret(2, g, prv).wait_send()
        ret(3, g, prv).wait_send()
        for c in ostore(g) + okv_store(g):
            c.wait()
        return carry

    lax.fori_loop(0, KVH, drain, 0)


def on_device(queries, key_rows, value_rows, grad_out, doc_lengths):
    hbm = pl.BlockSpec(memory_space=pl.ANY)
    dma = pltpu.SemaphoreType.DMA
    wide = jax.ShapeDtypeStruct((1, TOK, KVH * GW), BF16)
    narrow = jax.ShapeDtypeStruct((1, TOK, KVH * HD), BF16)
    o, dq, dk, dv, bias = pl.pallas_call(
        kernel,
        out_shape=(wide, wide, narrow, narrow, jax.ShapeDtypeStruct((28, HD), F32)),
        in_specs=[pl.BlockSpec(memory_space=pltpu.SMEM)] + [hbm] * 4,
        out_specs=[hbm] * 4 + [pl.BlockSpec(memory_space=pltpu.VMEM)],
        scratch_shapes=[
            pltpu.VMEM((TOK, KVH * GW), BF16),
            pltpu.VMEM((TOK, KVH * GW), BF16),
            pltpu.VMEM((TOK, KVH * GW), BF16),
            pltpu.VMEM((TOK, KVH * GW), BF16),
            pltpu.VMEM((KVH, 2, WIN, HD), BF16),
            pltpu.VMEM((KVH, 2, WIN, HD), F32),
            pltpu.VMEM((KVH, 4, 2, TOK, HD), BF16),
            pltpu.VMEM((KVH, 4, 2, TOK, HD), BF16),
            pltpu.VMEM((KVH, 2, TOK, HD), BF16),
            pltpu.VMEM((TOK, WIN), F32),
            pltpu.VMEM((HD, WIN), F32),
            pltpu.VMEM((HD, WIN), F32),
            pltpu.VMEM((KVH, 8, HD), F32),
            pltpu.VMEM((8, KVH, 8, HD), F32),
            pltpu.VMEM((4, KVH, 8, HD), F32),
            pltpu.VMEM((8, KVH, 8, HD), F32),
            dma((KVH, 2)),
            dma((KVH, 2)),
            dma((KVH, 2)),
            dma((KVH, 2)),
            dma((KVH, 5)),
            dma((KVH, 5)),
            dma((KVH, 4)),
            dma((KVH, 4)),
            dma((20,)),
            dma((8,)),
            dma((4,)),
            dma((8,)),
        ],
        compiler_params=pltpu.CompilerParams(
            collective_id=0, has_side_effects=True, vmem_limit_bytes=56 * 1024 * 1024
        ),
        cost_estimate=pl.CostEstimate(flops=10_000_000_000, bytes_accessed=8_000_000, transcendentals=6_000_000),
    )(doc_lengths, queries, key_rows, value_rows, grad_out)
    return o, dq, dk, dv, bias.reshape(28 * HD)


def solution(mesh):
    spec = P("dp", "ctx", None)
    return jax.shard_map(
        on_device,
        mesh=mesh,
        in_specs=(spec, spec, spec, spec, P("dp", None)),
        out_specs=(spec, spec, spec, spec, P()),
        check_vma=False,
    )
```

time: 517 us -> 80.5 us (0.16)
  the two profiles are of different devices: /device:TPU:32 before, /device:TPU:6 now
where the time goes in v1:
time: 80.5 us; the launch traced here: 80.2 us
  Pallas kernels  73.9 us (92%)
  local copies, waits for them, and re-layouts  5.65 us (7%)
    pallas_call x1, Pallas kernels, on_device(): pl.pallas_call(kernel, out_shape=(wide, wide, narrow, narrow, jax.ShapeDt...  73.9 us
    unnamed x13, local copies, waits for them, and re-layouts  5.65 us

profile of v1, /device:TPU:6, one launch (start us, length us, event | category | flops | bytes accessed | tf_op | source)
XLA Modules:
  0.0 80.2 jit_solution(877315499500259674)
XLA Ops:
  0.6 73.9 %shard_map.92 = (bf16[1,256,2560]{2,1,0:T(8,128)(2,1)}, bf16[1,256,2560]{2,1,0:T(8,128)(2,1)}, bf16[1,256,512]{2,1,0:T(8,128)(2,1)}, bf16[1,256,512]{2,1,0:T(8,128)(2,1)}, f32[28,128]{1,0:T(8,128)}) custom-call(s32[1,32]{1,0:T(1,128)} %lens.1, bf16[1,256,2560]{2,1,0:T(8,128)(2,1)} %q_hbm.1, bf16[1,256,512]{2,1,0:T(8,128)(2,1)} %k_hbm.1, ...), custom_call_target="tpu_custom_call" | custom-call | flops 10000000000 | bytes 8000000 | tf_op jit(solution)/shard_map/pallas_call | solution.py:423
  74.6 0.0 copy-start
  74.6 2.6 %copy.15 = bf16[1,256,2560]{2,1,0:T(8,128)(2,1)} copy(bf16[1,256,2560]{2,1,0:T(8,128)(2,1)} %get-tuple-element.20) | data formatting | bytes 2621440
  77.2 0.0 copy-done
  77.2 0.0 copy-start.2
  77.2 0.0 copy-start.1
  77.2 0.0 copy-start.3
  77.2 1.1 %copy.16 = bf16[1,256,2560]{2,1,0:T(8,128)(2,1)} copy(bf16[1,256,2560]{2,1,0:T(8,128)(2,1)S(1)} %copy-done) | data formatting | bytes 2621440
  78.2 0.0 copy-done.2
  78.2 0.7 copy.17
  78.9 0.0 copy-done.1
  78.9 0.7 copy.18
  79.6 0.0 copy-done.3
  79.6 0.6 copy.19
Async XLA Ops:
  74.6 2.6 %copy-start = (bf16[1,256,2560]{2,1,0:T(8,128)(2,1)S(1)}, bf16[1,256,2560]{2,1,0:T(8,128)(2,1)}, u32[]{:S(2)}) copy-start(bf16[1,256,2560]{2,1,0:T(8,128)(2,1)} %get-tuple-element.21) | copy-start | bytes 3932164
  77.2 1.1 %copy-start.2 = (bf16[1,256,512]{2,1,0:T(8,128)(2,1)S(1)}, bf16[1,256,512]{2,1,0:T(8,128)(2,1)}, u32[]{:S(2)}) copy-start(bf16[1,256,512]{2,1,0:T(8,128)(2,1)} %get-tuple-element.22) | copy-start | bytes 786436
  77.2 1.8 %copy-start.1 = (bf16[1,256,512]{2,1,0:T(8,128)(2,1)S(1)}, bf16[1,256,512]{2,1,0:T(8,128)(2,1)}, u32[]{:S(2)}) copy-start(bf16[1,256,512]{2,1,0:T(8,128)(2,1)} %get-tuple-element.23) | copy-start | bytes 786436
  77.2 2.5 %copy-start.3 = (f32[28,128]{1,0:T(8,128)S(1)}, f32[28,128]{1,0:T(8,128)}, u32[]{:S(2)}) copy-start(f32[28,128]{1,0:T(8,128)} %get-tuple-element.14) | copy-start | bytes 43012

commit v2 on v1

v2 whole, which is shorter than its diff:
```python
import math

import jax
import jax.numpy as jnp
from jax import lax
from jax.experimental import pallas as pl
from jax.experimental.pallas import tpu as pltpu
from jax.sharding import PartitionSpec as P

KVH = 4
HD = 128
GROUP = 5
TOK = 256
SPAN = 4
WIN = (SPAN + 1) * TOK
HALF = 128
HWIN = SPAN * TOK + HALF
GW = GROUP * HD
DOCS = 32
SCALE = 1.0 / math.sqrt(HD)
SCALE2 = SCALE * math.log2(math.e)
NT = (((1,), (1,)), ((), ()))
MESH = pl.DeviceIdType.MESH
F32 = jnp.float32
BF16 = jnp.bfloat16


def kernel(
    lens, q_hbm, k_hbm, v_hbm, do_hbm,
    ob, dqb, dk_out, dv_out, bias_out,
    q, do, kv, part, stage, got, mask, dkt, dvt, wkeep, lowkeep, stat,
    sums, b1, b2, b3,
    load_sem, kv_sem,
    fs, fr, rs, rr, bs, br1, br2, br3,
):
    dp = lax.axis_index("dp")
    me = lax.axis_index("ctx")
    n = 64
    core = lax.rem(me, 2)
    nxt = lax.rem(me + 2, n)
    prv = lax.rem(me + n - 2, n)
    mate = me + 1 - 2 * core
    rank1 = lax.rem(me, 8)
    rank2 = lax.rem(me // 8, 4)
    zlo = me // 32
    rank3 = dp * 2 + zlo

    def peer1(d):
        return (dp, me - rank1 + lax.rem(rank1 + d, 8))

    def peer2(d):
        return (dp, me + 8 * (lax.rem(rank2 + d, 4) - rank2))

    def peer3(d):
        r = lax.rem(rank3 + d, 8)
        return (r // 2, me + 32 * (lax.rem(r, 2) - zlo))

    def kvload(g):
        c = g * HD
        return (
            pltpu.make_async_copy(k_hbm.at[0, :, pl.ds(c, HD)], kv.at[g, 0, pl.ds(SPAN * TOK, TOK)], kv_sem.at[g, 0]),
            pltpu.make_async_copy(v_hbm.at[0, :, pl.ds(c, HD)], kv.at[g, 1, pl.ds(SPAN * TOK, TOK)], kv_sem.at[g, 1]),
        )

    def qload(g):
        c = pl.ds(pl.multiple_of(g * GW, 128), GW)
        return (
            pltpu.make_async_copy(q_hbm.at[0, :, c], q.at[:, c], load_sem.at[g, 0]),
            pltpu.make_async_copy(do_hbm.at[0, :, c], do.at[:, c], load_sem.at[g, 1]),
        )

    def fwd(kind, g, t, src_slot, dst_slot, to):
        return pltpu.make_async_remote_copy(
            src_ref=kv.at[g, t, pl.ds(src_slot * TOK, TOK)],
            dst_ref=kv.at[g, t, pl.ds(dst_slot * TOK, TOK)],
            send_sem=fs.at[g, kind, t],
            recv_sem=fr.at[g, kind, t],
            device_id=(dp, to),
            device_id_type=MESH,
        )

    def h1(g, t):
        return fwd(0, g, t, 4, 2, nxt)

    def h2(g, t):
        return fwd(1, g, t, 2, 0, nxt)

    def l1(g, t):
        return fwd(2, g, t, 4, 3, mate)

    def l2_from0(g, t):
        return fwd(3, g, t, 2, 1, mate)

    def l2_from1(g, t):
        return fwd(3, g, t, 2, 3, mate)

    def l3(g, t):
        return fwd(4, g, t, 0, 1, mate)

    def near(g, t):
        h1(g, t).wait_recv()
        h2(g, t).start()

        @pl.when(core == 0)
        def _():
            l2_from0(g, t).start()

        @pl.when(core == 1)
        def _():
            l2_from1(g, t).start()

    def far(g, t):
        h2(g, t).wait_recv()

        @pl.when(core == 1)
        def _():
            l3(g, t).start()

    def complete(g):
        @pl.when(core == 0)
        def _():
            for t in range(2):
                l2_from1(g, t).wait_recv()
                l3(g, t).wait_recv()

        @pl.when(core == 1)
        def _():
            for t in range(2):
                l1(g, t).wait_recv()
                l2_from0(g, t).wait_recv()

    def mate_send(g):
        @pl.when(core == 0)
        def _():
            for t in range(2):
                l1(g, t).start()

    def ret(kind, g, t, to):
        return pltpu.make_async_remote_copy(
            src_ref=stage.at[g, kind, t],
            dst_ref=got.at[g, kind, t],
            send_sem=rs.at[g, kind, t],
            recv_sem=rr.at[g, kind, t],
            device_id=(dp, to),
            device_id_type=MESH,
        )

    def r1(g, t):
        for kind, slot in ((0, 1), (1, 3)):
            stage[g, kind, t] = part[g, t, slot * TOK:(slot + 1) * TOK].astype(BF16)
            ret(kind, g, t, mate).start()

    def r2(g, t):
        ret(0, g, t, mate).wait_recv()

        @pl.when(core == 0)
        def _():
            stage[g, 2, t] = part[g, t, 0:TOK].astype(BF16)

        @pl.when(core == 1)
        def _():
            stage[g, 2, t] = (part[g, t, 0:TOK] + got[g, 0, t].astype(F32)).astype(BF16)

        ret(2, g, t, prv).start()
        ret(1, g, t, mate).wait_recv()

        @pl.when(core == 0)
        def _():
            part[g, t, 2 * TOK:3 * TOK] += got[g, 0, t].astype(F32)
            part[g, t, 4 * TOK:] += got[g, 1, t].astype(F32)

        @pl.when(core == 1)
        def _():
            part[g, t, 2 * TOK:3 * TOK] += got[g, 1, t].astype(F32)

    def r3(g, t):
        ret(2, g, t, prv).wait_recv()
        stage[g, 3, t] = (part[g, t, 2 * TOK:3 * TOK] + got[g, 2, t].astype(F32)).astype(BF16)
        ret(3, g, t, prv).start()

    def r4(g, t):
        ret(3, g, t, prv).wait_recv()
        c = pl.ds(pl.multiple_of(g * HD, 128), HD)
        (dk_out, dv_out)[t][0, :, c] = (part[g, t, 4 * TOK:] + got[g, 3, t].astype(F32)).astype(BF16)

    def bias_send(buf, rank, peer, size, sem_at, recv):
        for d in range(1, size):
            pltpu.make_async_remote_copy(
                src_ref=buf.at[rank],
                dst_ref=buf.at[rank],
                send_sem=bs.at[sem_at + d],
                recv_sem=recv.at[rank],
                device_id=peer(d),
                device_id_type=MESH,
            ).start()

    def bias_wait(buf, rank, peer, size, sem_at, recv):
        for d in range(1, size):
            other = lax.rem(rank + d, size)
            pltpu.make_async_remote_copy(
                src_ref=buf.at[rank],
                dst_ref=buf.at[other],
                send_sem=bs.at[sem_at + d],
                recv_sem=recv.at[other],
                device_id=peer(d),
                device_id_type=MESH,
            ).wait()
        total = buf[0]
        for r in range(1, size):
            total = total + buf[r]
        return total

    for g in range(KVH):
        for c in kvload(g):
            c.start()
    for g in range(KVH):
        for c in qload(g):
            c.start()

    barrier = pltpu.get_barrier_semaphore()
    peers = [(dp, nxt), (dp, prv)]
    peers += [peer1(d) for d in range(1, 8)]
    peers += [peer2(d) for d in range(1, 4)]
    peers += [peer3(d) for d in range(1, 8)]
    for p in peers:
        pl.semaphore_signal(barrier, inc=1, device_id=p, device_id_type=MESH)
    pl.semaphore_wait(barrier, len(peers))

    for t in range(2):
        kvload(0)[t].wait()
        h1(0, t).start()
    mate_send(0)
    for g in range(1, KVH):
        for c in kvload(g):
            c.wait()
        mate_send(g)
    for t in range(2):
        h1(0, t).wait_send()
        h1(1, t).start()

    where = me * TOK
    t_pos = lax.broadcasted_iota(jnp.int32, (TOK, 128), 0) + where
    first = jnp.zeros((TOK, 128), jnp.int32)
    bound = jnp.int32(0)
    for i in range(DOCS):
        bound = bound + lens[0, i]
        first = jnp.where(t_pos >= bound, bound, first)
    for c in range(WIN // 128):
        s_pos = lax.broadcasted_iota(jnp.int32, (TOK, 128), 1) + (where - SPAN * TOK + c * 128)
        mask[:, c * 128:(c + 1) * 128] = jnp.where((s_pos >= first) & (s_pos <= t_pos), 0.0, -1e30).astype(F32)

    for t in range(2):
        near(0, t)
    for t in range(2):
        near(1, t)
    for t in range(2):
        far(0, t)
    for t in range(2):
        h1(2, t).start()

    def stacked(g, h, of):
        rows = slice(h * HALF, (h + 1) * HALF)
        return jnp.concatenate([of[rows, c] for c in columns(g)], 0)

    def columns(g):
        return [pl.ds(pl.multiple_of(g * GW + j * HD, 128), HD) for j in range(GROUP)]

    def unit_a(g, h):
        w0 = h * HALF
        rows = slice(w0, w0 + HALF)
        K = kv[g, 0, w0:w0 + HWIN]
        V = kv[g, 1, w0:w0 + HWIN]
        Q = stacked(g, h, q)
        D = stacked(g, h, do)
        bias = jnp.concatenate([mask[rows, w0:w0 + HWIN]] * GROUP, 0)
        s = lax.dot_general(Q, K, NT, preferred_element_type=F32) * SCALE2 + bias
        m = jnp.max(s, axis=1, keepdims=True)
        w = jnp.exp2(s - m)
        inv = 1.0 / jnp.sum(w, axis=1, keepdims=True)
        low = (w * inv).astype(BF16)
        o = jnp.dot(low, V, preferred_element_type=F32).astype(BF16)
        delta = jnp.sum(D.astype(F32) * o.astype(F32), axis=1, keepdims=True)
        for j, c in enumerate(columns(g)):
            ob[0, rows, c] = o[j * HALF:(j + 1) * HALF]
        wkeep[...] = w
        lowkeep[...] = low
        stat[:, 0:128] = jnp.broadcast_to(inv * SCALE, (GROUP * HALF, 128))
        stat[:, 128:256] = jnp.broadcast_to(delta, (GROUP * HALF, 128))

    def unit_b(g, h):
        w0 = h * HALF
        rows = slice(w0, w0 + HALF)
        K = kv[g, 0, w0:w0 + HWIN]
        V = kv[g, 1, w0:w0 + HWIN]
        Q = stacked(g, h, q)
        D = stacked(g, h, do)
        dprobs = lax.dot_general(D, V, NT, preferred_element_type=F32)
        a2 = jnp.dot(D.T, lowkeep[...], preferred_element_type=F32)
        if h == 0:
            dvt[:, :HWIN] = a2
            dvt[:, HWIN:] = jnp.zeros((HD, WIN - HWIN), F32)
        else:
            dvt[:, w0:] += a2
        ds = ((wkeep[...] * stat[:, 0:1]) * (dprobs - stat[:, 128:129])).astype(BF16)
        dq = jnp.dot(ds, K, preferred_element_type=F32)
        for j, c in enumerate(columns(g)):
            dqj = dq[j * HALF:(j + 1) * HALF]
            dqb[0, rows, c] = dqj.astype(BF16)
            dqs = jnp.sum(dqj, axis=0, keepdims=True)
            if h == 0:
                sums[g, j:j + 1] = dqs
            else:
                sums[g, j:j + 1] += dqs
        a1 = jnp.dot(Q.T, ds, preferred_element_type=F32)
        if h == 0:
            dkt[:, :HWIN] = a1
            dkt[:, HWIN:] = jnp.zeros((HD, WIN - HWIN), F32)
        else:
            dkt[:, w0:] += a1

    def unit(g):
        w0 = HALF
        rows = slice(w0, w0 + HALF)
        K = kv[g, 0, w0:w0 + HWIN]
        V = kv[g, 1, w0:w0 + HWIN]
        Q = stacked(g, 1, q)
        D = stacked(g, 1, do)
        bias = jnp.concatenate([mask[rows, w0:w0 + HWIN]] * GROUP, 0)
        s = lax.dot_general(Q, K, NT, preferred_element_type=F32) * SCALE2 + bias
        dprobs = lax.dot_general(D, V, NT, preferred_element_type=F32)
        m = jnp.max(s, axis=1, keepdims=True)
        w = jnp.exp2(s - m)
        inv = 1.0 / jnp.sum(w, axis=1, keepdims=True)
        low = (w * inv).astype(BF16)
        o = jnp.dot(low, V, preferred_element_type=F32).astype(BF16)
        delta = jnp.sum(D.astype(F32) * o.astype(F32), axis=1, keepdims=True)
        ds = ((w * (inv * SCALE)) * (dprobs - delta)).astype(BF16)
        dvt[:, w0:] += jnp.dot(D.T, low, preferred_element_type=F32)
        dv = dvt[...].T
        part[g, 1] = dv
        sums[g, 6:7] = jnp.sum(dv, axis=0, keepdims=True)
        r1(g, 1)
        dq = jnp.dot(ds, K, preferred_element_type=F32)
        for j, c in enumerate(columns(g)):
            ob[0, rows, c] = o[j * HALF:(j + 1) * HALF]
            dqj = dq[j * HALF:(j + 1) * HALF]
            dqb[0, rows, c] = dqj.astype(BF16)
            sums[g, j:j + 1] += jnp.sum(dqj, axis=0, keepdims=True)
        dkt[:, w0:] += jnp.dot(Q.T, ds, preferred_element_type=F32)

    def finish(g):
        dk = dkt[...].T
        part[g, 0] = dk
        r1(g, 0)
        sums[g, 5:6] = jnp.sum(dk, axis=0, keepdims=True)
        sums[g, 7:8] = jnp.zeros((1, HD), F32)

    def both(step, g):
        step(g, 1)
        step(g, 0)

    def body(g, carry):
        complete(g)
        for c in qload(g):
            c.wait()
        unit_a(g, 0)

        @pl.when(g > 0)
        def _():
            both(r2, g - 1)

        @pl.when((g > 0) & (g < 3))
        def _():
            both(far, g + 1)

        unit_b(g, 0)

        @pl.when(g == 0)
        def _():
            both(far, 1)
            both(near, 2)
            for t in range(2):
                h1(3, t).start()

        @pl.when(g == 1)
        def _():
            both(near, 3)

        unit(g)

        @pl.when(g > 0)
        def _():
            both(r3, g - 1)

        @pl.when(g == 3)
        def _():
            r2(g, 1)

        finish(g)

        @pl.when(g > 1)
        def _():
            both(r4, g - 2)

        return carry

    lax.fori_loop(0, KVH, body, 0)

    b1[rank1] = sums[...]
    bias_send(b1, rank1, peer1, 8, 0, br1)
    r2(3, 0)
    r3(3, 1)
    total = bias_wait(b1, rank1, peer1, 8, 0, br1)
    b2[rank2] = total
    bias_send(b2, rank2, peer2, 4, 8, br2)
    r3(3, 0)
    total = bias_wait(b2, rank2, peer2, 4, 8, br2)
    b3[rank3] = total
    bias_send(b3, rank3, peer3, 8, 12, br3)
    both(r4, 2)
    both(r4, 3)
    total = bias_wait(b3, rank3, peer3, 8, 12, br3)
    for g in range(KVH):
        bias_out[g * GROUP:(g + 1) * GROUP] = total[g, 0:GROUP]
        bias_out[20 + g:21 + g] = total[g, 5:6]
        bias_out[24 + g:25 + g] = total[g, 6:7]

    def drain(g, carry):
        @pl.when(g > 0)
        def _():
            for t in range(2):
                h1(g, t).wait_send()

        for t in range(2):
            h2(g, t).wait_send()

        @pl.when(core == 0)
        def _():
            for t in range(2):
                l1(g, t).wait_send()
                l2_from0(g, t).wait_send()

        @pl.when(core == 1)
        def _():
            for t in range(2):
                l2_from1(g, t).wait_send()
                l3(g, t).wait_send()

        for t in range(2):
            ret(0, g, t, mate).wait_send()
            ret(1, g, t, mate).wait_send()
            ret(2, g, t, prv).wait_send()
            ret(3, g, t, prv).wait_send()
        return carry

    lax.fori_loop(0, KVH, drain, 0)


def on_device(queries, key_rows, value_rows, grad_out, doc_lengths):
    hbm = pl.BlockSpec(memory_space=pl.ANY)
    vmem = pl.BlockSpec(memory_space=pltpu.VMEM)
    dma = pltpu.SemaphoreType.DMA
    shapes = [((1, TOK, KVH * GW), BF16)] * 2 + [((1, TOK, KVH * HD), BF16)] * 2 + [((28, HD), F32)]
    held = pl.pallas_call(
        kernel,
        out_shape=[pltpu.VMEM(*a) for a in shapes],
        in_specs=[pl.BlockSpec(memory_space=pltpu.SMEM)] + [hbm] * 4,
        out_specs=[vmem] * 5,
        scratch_shapes=[
            pltpu.VMEM((TOK, KVH * GW), BF16),
            pltpu.VMEM((TOK, KVH * GW), BF16),
            pltpu.VMEM((KVH, 2, WIN, HD), BF16),
            pltpu.VMEM((KVH, 2, WIN, HD), F32),
            pltpu.VMEM((KVH, 4, 2, TOK, HD), BF16),
            pltpu.VMEM((KVH, 4, 2, TOK, HD), BF16),
            pltpu.VMEM((TOK, WIN), F32),
            pltpu.VMEM((HD, WIN), F32),
            pltpu.VMEM((HD, WIN), F32),
            pltpu.VMEM((GROUP * HALF, HWIN), F32),
            pltpu.VMEM((GROUP * HALF, HWIN), BF16),
            pltpu.VMEM((GROUP * HALF, 256), F32),
            pltpu.VMEM((KVH, 8, HD), F32),
            pltpu.VMEM((8, KVH, 8, HD), F32),
            pltpu.VMEM((4, KVH, 8, HD), F32),
            pltpu.VMEM((8, KVH, 8, HD), F32),
            dma((KVH, 2)),
            dma((KVH, 2)),
            dma((KVH, 5, 2)),
            dma((KVH, 5, 2)),
            dma((KVH, 4, 2)),
            dma((KVH, 4, 2)),
            dma((20,)),
            dma((8,)),
            dma((4,)),
            dma((8,)),
        ],
        compiler_params=pltpu.CompilerParams(
            collective_id=0, has_side_effects=True, vmem_limit_bytes=54 * 1024 * 1024
        ),
        cost_estimate=pl.CostEstimate(flops=10_000_000_000, bytes_accessed=8_000_000, transcendentals=6_000_000),
    )(doc_lengths, queries, key_rows, value_rows, grad_out)
    o, dq, dk, dv, bias = held
    return o, dq, dk, dv, bias.reshape(28 * HD)


def solution(mesh):
    spec = P("dp", "ctx", None)
    return jax.shard_map(
        on_device,
        mesh=mesh,
        in_specs=(spec, spec, spec, spec, P("dp", None)),
        out_specs=(spec, spec, spec, spec, P()),
        check_vma=False,
    )
```

time: 80.5 us -> 77 us (0.957)
  Pallas kernels: 73.9 us -> 72.1 us
  local copies, waits for them, and re-layouts: 5.65 us -> 4.13 us
    pallas_call x1, Pallas kernels: 73.9 us -> 72.1 us  [on_device(): pl.pallas_call(kernel, out_shape=[pltpu.VMEM(*a) for a in shapes], in_spe...]
    unnamed x13 -> x5, local copies, waits for them, and re-layouts: 5.65 us -> 4.13 us
where the time goes in v2:
time: 77 us; the launch traced here: 76.9 us
  Pallas kernels  72.1 us (94%)
  local copies, waits for them, and re-layouts  4.13 us (5%)
    pallas_call x1, Pallas kernels, on_device(): pl.pallas_call(kernel, out_shape=[pltpu.VMEM(*a) for a in shapes], in_spe...  72.1 us
    unnamed x5, local copies, waits for them, and re-layouts  4.13 us

profile of v2, /device:TPU:6, one launch (start us, length us, event | category | flops | bytes accessed | tf_op | source)
XLA Modules:
  0.0 76.9 jit_solution(6532556225180682083)
XLA Ops:
  0.6 72.1 %shard_map.92 = (bf16[1,256,2560]{2,1,0:T(8,128)(2,1)S(1)}, bf16[1,256,2560]{2,1,0:T(8,128)(2,1)S(1)}, bf16[1,256,512]{2,1,0:T(8,128)(2,1)S(1)}, bf16[1,256,512]{2,1,0:T(8,128)(2,1)S(1)}, f32[28,128]{1,0:T(8,128)S(1)}) custom-call(s32[1,32]{1,0:T(1,128)} %lens.1, bf16[1,256,2560]{2,1,0:T(8,128)(2,1)} %q_hbm.1, bf16[1,256,512]{2,1,0:T(8,128)(2,1)} %k_hbm.1, ...), custom_call_target="tpu_custom_call" | custom-call | flops 10000000000 | bytes 8000000 | tf_op jit(solution)/shard_map/pallas_call | solution.py:464
  72.8 1.1 %copy.15 = bf16[1,256,2560]{2,1,0:T(8,128)(2,1)} copy(bf16[1,256,2560]{2,1,0:T(8,128)(2,1)S(1)} %get-tuple-element.15) | data formatting | bytes 2621440
  73.8 0.6 copy.19
  74.5 0.7 copy.17
  75.2 0.7 copy.18
  75.9 1.1 %copy.16 = bf16[1,256,2560]{2,1,0:T(8,128)(2,1)} copy(bf16[1,256,2560]{2,1,0:T(8,128)(2,1)S(1)} %get-tuple-element.16) | data formatting | bytes 2621440

commit v3 on v2

--- a/solution.py
+++ b/solution.py
@@ -28,7 +28,7 @@
 def kernel(
     lens, q_hbm, k_hbm, v_hbm, do_hbm,
     ob, dqb, dk_out, dv_out, bias_out,
-    q, do, kv, part, stage, got, mask, dkt, dvt, wkeep, lowkeep, stat,
+    q, do, kv, part, stage, got, mask, dkt, dvt, pkeep, lowkeep, stat,
     sums, b1, b2, b3,
     load_sem, kv_sem,
     fs, fr, rs, rr, bs, br1, br2, br3,
@@ -277,15 +277,15 @@
         m = jnp.max(s, axis=1, keepdims=True)
         w = jnp.exp2(s - m)
         inv = 1.0 / jnp.sum(w, axis=1, keepdims=True)
-        low = (w * inv).astype(BF16)
+        p = w * inv
+        low = p.astype(BF16)
         o = jnp.dot(low, V, preferred_element_type=F32).astype(BF16)
         delta = jnp.sum(D.astype(F32) * o.astype(F32), axis=1, keepdims=True)
         for j, c in enumerate(columns(g)):
             ob[0, rows, c] = o[j * HALF:(j + 1) * HALF]
-        wkeep[...] = w
+        pkeep[...] = p
         lowkeep[...] = low
-        stat[:, 0:128] = jnp.broadcast_to(inv * SCALE, (GROUP * HALF, 128))
-        stat[:, 128:256] = jnp.broadcast_to(delta, (GROUP * HALF, 128))
+        stat[...] = jnp.broadcast_to(delta, (GROUP * HALF, 128))
 
     def unit_b(g, h):
         w0 = h * HALF
@@ -301,7 +301,7 @@
             dvt[:, HWIN:] = jnp.zeros((HD, WIN - HWIN), F32)
         else:
             dvt[:, w0:] += a2
-        ds = ((wkeep[...] * stat[:, 0:1]) * (dprobs - stat[:, 128:129])).astype(BF16)
+        ds = ((pkeep[...] * SCALE) * (dprobs - stat[:, 0:1])).astype(BF16)
         dq = jnp.dot(ds, K, preferred_element_type=F32)
         for j, c in enumerate(columns(g)):
             dqj = dq[j * HALF:(j + 1) * HALF]
@@ -327,14 +327,15 @@
         D = stacked(g, 1, do)
         bias = jnp.concatenate([mask[rows, w0:w0 + HWIN]] * GROUP, 0)
         s = lax.dot_general(Q, K, NT, preferred_element_type=F32) * SCALE2 + bias
-        dprobs = lax.dot_general(D, V, NT, preferred_element_type=F32)
         m = jnp.max(s, axis=1, keepdims=True)
         w = jnp.exp2(s - m)
         inv = 1.0 / jnp.sum(w, axis=1, keepdims=True)
-        low = (w * inv).astype(BF16)
+        p = w * inv
+        low = p.astype(BF16)
         o = jnp.dot(low, V, preferred_element_type=F32).astype(BF16)
+        dprobs = lax.dot_general(D, V, NT, preferred_element_type=F32)
         delta = jnp.sum(D.astype(F32) * o.astype(F32), axis=1, keepdims=True)
-        ds = ((w * (inv * SCALE)) * (dprobs - delta)).astype(BF16)
+        ds = ((p * SCALE) * (dprobs - delta)).astype(BF16)
         dvt[:, w0:] += jnp.dot(D.T, low, preferred_element_type=F32)
         dv = dvt[...].T
         part[g, 1] = dv
@@ -388,17 +389,13 @@
 
         unit(g)
 
-        @pl.when(g > 0)
+        finish(g)
+
+        @pl.when((g > 0) & (g < 3))
         def _():
             both(r3, g - 1)
 
-        @pl.when(g == 3)
-        def _():
-            r2(g, 1)
-
-        finish(g)
-
-        @pl.when(g > 1)
+        @pl.when(g == 2)
         def _():
             both(r4, g - 2)
 
@@ -408,15 +405,16 @@
 
     b1[rank1] = sums[...]
     bias_send(b1, rank1, peer1, 8, 0, br1)
-    r2(3, 0)
-    r3(3, 1)
+    both(r2, 3)
+    both(r3, 2)
     total = bias_wait(b1, rank1, peer1, 8, 0, br1)
     b2[rank2] = total
     bias_send(b2, rank2, peer2, 4, 8, br2)
-    r3(3, 0)
+    both(r3, 3)
     total = bias_wait(b2, rank2, peer2, 4, 8, br2)
     b3[rank3] = total
     bias_send(b3, rank3, peer3, 8, 12, br3)
+    both(r4, 1)
     both(r4, 2)
     both(r4, 3)
     total = bias_wait(b3, rank3, peer3, 8, 12, br3)
@@ -478,7 +476,7 @@
             pltpu.VMEM((HD, WIN), F32),
             pltpu.VMEM((GROUP * HALF, HWIN), F32),
             pltpu.VMEM((GROUP * HALF, HWIN), BF16),
-            pltpu.VMEM((GROUP * HALF, 256), F32),
+            pltpu.VMEM((GROUP * HALF, 128), F32),
             pltpu.VMEM((KVH, 8, HD), F32),
             pltpu.VMEM((8, KVH, 8, HD), F32),
             pltpu.VMEM((4, KVH, 8, HD), F32),

time: 77 us -> 76.4 us (level)
  no operation moved by 1% of the time
where the time goes in v3:
time: 76.4 us; the launch traced here: 76.2 us
  Pallas kernels  71.5 us (94%)
  local copies, waits for them, and re-layouts  4.13 us (5%)
    pallas_call x1, Pallas kernels, on_device(): pl.pallas_call(kernel, out_shape=[pltpu.VMEM(*a) for a in shapes], in_spe...  71.5 us
    unnamed x5, local copies, waits for them, and re-layouts  4.13 us

profile of v3, /device:TPU:6, one launch (start us, length us, event | category | flops | bytes accessed | tf_op | source)
XLA Modules:
  0.0 76.2 jit_solution(5611085606340767359)
XLA Ops:
  0.6 71.5 %shard_map.92 = (bf16[1,256,2560]{2,1,0:T(8,128)(2,1)S(1)}, bf16[1,256,2560]{2,1,0:T(8,128)(2,1)S(1)}, bf16[1,256,512]{2,1,0:T(8,128)(2,1)S(1)}, bf16[1,256,512]{2,1,0:T(8,128)(2,1)S(1)}, f32[28,128]{1,0:T(8,128)S(1)}) custom-call(s32[1,32]{1,0:T(1,128)} %lens.1, bf16[1,256,2560]{2,1,0:T(8,128)(2,1)} %q_hbm.1, bf16[1,256,512]{2,1,0:T(8,128)(2,1)} %k_hbm.1, ...), custom_call_target="tpu_custom_call" | custom-call | flops 10000000000 | bytes 8000000 | tf_op jit(solution)/shard_map/pallas_call | solution.py:462
  72.1 1.1 %copy.15 = bf16[1,256,2560]{2,1,0:T(8,128)(2,1)} copy(bf16[1,256,2560]{2,1,0:T(8,128)(2,1)S(1)} %get-tuple-element.15) | data formatting | bytes 2621440
  73.2 0.6 copy.19
  73.8 0.7 copy.17
  74.5 0.7 copy.18
  75.2 1.1 %copy.16 = bf16[1,256,2560]{2,1,0:T(8,128)(2,1)} copy(bf16[1,256,2560]{2,1,0:T(8,128)(2,1)S(1)} %get-tuple-element.16) | data formatting | bytes 2621440

commit v4 on v3

--- a/solution.py
+++ b/solution.py
@@ -352,9 +352,15 @@
     def finish(g):
         dk = dkt[...].T
         part[g, 0] = dk
-        r1(g, 0)
         sums[g, 5:6] = jnp.sum(dk, axis=0, keepdims=True)
         sums[g, 7:8] = jnp.zeros((1, HD), F32)
+
+        @pl.when(g == 3)
+        def _():
+            b1[rank1] = sums[...]
+            bias_send(b1, rank1, peer1, 8, 0, br1)
+
+        r1(g, 0)
 
     def both(step, g):
         step(g, 1)
@@ -403,8 +409,6 @@
 
     lax.fori_loop(0, KVH, body, 0)
 
-    b1[rank1] = sums[...]
-    bias_send(b1, rank1, peer1, 8, 0, br1)
     both(r2, 3)
     both(r3, 2)
     total = bias_wait(b1, rank1, peer1, 8, 0, br1)

time: 76.4 us -> 76.6 us (level)
  no operation moved by 1% of the time
where the time goes in v4:
time: 76.6 us; the launch traced here: 76.4 us
  Pallas kernels  71.6 us (93%)
  local copies, waits for them, and re-layouts  4.13 us (5%)
    pallas_call x1, Pallas kernels, on_device(): pl.pallas_call(kernel, out_shape=[pltpu.VMEM(*a) for a in shapes], in_spe...  71.6 us
    unnamed x5, local copies, waits for them, and re-layouts  4.13 us

profile of v4, /device:TPU:6, one launch (start us, length us, event | category | flops | bytes accessed | tf_op | source)
XLA Modules:
  0.0 76.4 jit_solution(8624852659784368697)
XLA Ops:
  0.6 71.6 %shard_map.92 = (bf16[1,256,2560]{2,1,0:T(8,128)(2,1)S(1)}, bf16[1,256,2560]{2,1,0:T(8,128)(2,1)S(1)}, bf16[1,256,512]{2,1,0:T(8,128)(2,1)S(1)}, bf16[1,256,512]{2,1,0:T(8,128)(2,1)S(1)}, f32[28,128]{1,0:T(8,128)S(1)}) custom-call(s32[1,32]{1,0:T(1,128)} %lens.1, bf16[1,256,2560]{2,1,0:T(8,128)(2,1)} %q_hbm.1, bf16[1,256,512]{2,1,0:T(8,128)(2,1)} %k_hbm.1, ...), custom_call_target="tpu_custom_call" | custom-call | flops 10000000000 | bytes 8000000 | tf_op jit(solution)/shard_map/pallas_call | solution.py:466
  72.2 1.1 %copy.15 = bf16[1,256,2560]{2,1,0:T(8,128)(2,1)} copy(bf16[1,256,2560]{2,1,0:T(8,128)(2,1)S(1)} %get-tuple-element.15) | data formatting | bytes 2621440
  73.3 0.6 copy.19
  73.9 0.7 copy.17
  74.6 0.7 copy.18
  75.3 1.1 %copy.16 = bf16[1,256,2560]{2,1,0:T(8,128)(2,1)} copy(bf16[1,256,2560]{2,1,0:T(8,128)(2,1)S(1)} %get-tuple-element.16) | data formatting | bytes 2621440
